TPU v7x, 128 devices: a whole 4x4x4 slice. The times are simulated.
128 devices in a mesh: tm: 32 (over x, z, core), state: 4 (over y).
Axes of the slice: x: 4, y: 4, z: 4, core: 2. Of those that a mesh axis runs over, the one named last changes fastest.
Arguments:
- dyn_cols: int32 [1024, 8, 3], P('tm', 'state'), may hold values from 0 to 7, as said below
- dyn_vals: bfloat16 [1024, 8, 64, 192], P('tm', 'state'), may hold values from -1 to 1
- obs_blocks: int32 [1024, 2], P('tm'), may hold values from 0 to 7
- obs_op: bfloat16 [1024, 64, 128], P('tm'), may hold values from -0.75 to 0.75
- obs_counts: int32 [1024], P('tm'), may hold values from 32 to 128, as said below
- obs_values: float32 [1024, 128], P('tm'), may hold values from -6 to 6
- gain: bfloat16 [1024, 512, 128], P('tm', 'state'), may hold values from -0.0078125 to 0.0078125
- sources: float32 [1024, 512], P('tm', 'state'), may hold values from -0.625 to 0.625
- prior: float32 [512], replicated, may hold values from -6 to 6
Outputs:
- filtered: float32 [1024, 512], P('tm', 'state')
Inputs may be any that keep to these rules, and one draw needn't show every extreme that they name: `dyn_cols`: for every step and block row i, the first entry is i itself and the 3 entries are distinct block columns. `obs_counts`: some step has all 128 observations present.
All inputs are finite; a program needn't handle non-finite values.
Results may differ from a plain program's by a relative error of at most 0.0003.
The roundings to bfloat16 on the way count: a program that leaves them out, or rounds other values in their place, can miss the bound.
Values may be sent and summed in bfloat16 or wider, within the bound.
A program may use at most 128 MiB of HBM per device.

v0:
```python
import jax
import jax.numpy as jnp
from jax import lax
from jax.sharding import PartitionSpec as P

NS = 512
BS = 64
KF = 3
OBS = 128
NB = 8
OB = 2
HIGHEST = lax.Precision.HIGHEST


def prefix(value, axis, join, neutral):
    count, mine = (lax.axis_size(axis), lax.axis_index(axis))
    pieces = jax.tree.map(lambda part: lax.all_gather(part, axis), value)
    so_far = jax.tree.map(
        lambda part, zero: jnp.full_like(part, 0) + jnp.asarray(zero, part.dtype), value, neutral
    )

    def step(position, so_far):
        longer = join(so_far, jax.tree.map(lambda part: part[position], pieces))
        return jax.tree.map(lambda new, old: jnp.where(position < mine, new, old), longer, so_far)

    return lax.fori_loop(0, count - 1, step, so_far)


def split_product(matrix, operand):
    leading = operand.astype(jnp.bfloat16)
    remainder = (operand - lax.optimization_barrier(leading).astype(jnp.float32)).astype(
        jnp.bfloat16
    )
    return jnp.dot(matrix, leading, preferred_element_type=jnp.float32) + jnp.dot(
        matrix, remainder, preferred_element_type=jnp.float32
    )


def body(dyn_cols, dyn_vals, obs_blocks, obs_op, obs_counts, obs_values, gain, sources, prior):
    step_count = dyn_vals.shape[0]
    local_blocks = dyn_vals.shape[1]
    local_rows = local_blocks * BS
    state_index = lax.axis_index("state")
    onehot = (dyn_cols[..., None] == jnp.arange(NB)).astype(jnp.bfloat16)
    blocks = dyn_vals.reshape(step_count, local_blocks, BS, KF, BS)
    forward = jnp.einsum("tikc,tiakb->tiacb", onehot, blocks, preferred_element_type=jnp.float32)
    forward = forward.reshape(step_count, local_blocks, BS, NS)
    forward_narrow = forward.astype(jnp.bfloat16)
    owned = state_index * local_blocks + jnp.arange(local_blocks)
    select = obs_blocks[:, :, None] == owned[None, None, :]
    selected = jnp.einsum(
        "tos,tsbn->tobn",
        select.astype(jnp.bfloat16),
        forward_narrow,
        preferred_element_type=jnp.float32,
    ).astype(jnp.bfloat16)
    operator_blocks = obs_op.reshape(step_count, BS, OB, BS)
    image_part = jnp.einsum(
        "tboa,tobn->toan", operator_blocks, selected, preferred_element_type=jnp.float32
    )
    image_part = image_part.reshape(step_count, OBS, NS)
    source_sel = jnp.einsum(
        "tos,tsb->tob",
        select.astype(jnp.float32),
        sources.reshape(step_count, local_blocks, BS),
        precision=HIGHEST,
    )
    source_part = jnp.einsum(
        "tboa,tob->toa", operator_blocks.astype(jnp.float32), source_sel, precision=HIGHEST
    )
    source_part = source_part.reshape(step_count, OBS)
    image_sum, source_sum = (
        lax.psum(image_part.astype(jnp.bfloat16), "state").astype(jnp.float32),
        lax.psum(source_part.astype(jnp.bfloat16), "state").astype(jnp.float32),
    )
    active = jnp.arange(OBS)[None, :] < obs_counts[:, None]
    masked = jnp.where(
        active[:, :, None], image_sum.astype(jnp.bfloat16), jnp.zeros((), jnp.bfloat16)
    )
    source_image = lax.optimization_barrier(source_sum.astype(jnp.bfloat16)).astype(jnp.float32)
    innovation = jnp.where(active, obs_values - source_image, 0.0)
    correction = jnp.einsum("tro,ton->trn", gain, masked, preferred_element_type=jnp.float32)
    element = (forward.reshape(step_count, local_rows, NS) - correction).astype(jnp.bfloat16)
    offset = sources + jnp.einsum(
        "tro,to->tr", gain.astype(jnp.float32), innovation, precision=HIGHEST
    )
    full_elements = lax.all_gather(element, "state", axis=1, tiled=True)
    full_offsets = lax.all_gather(offset, "state", axis=1, tiled=True)
    start_cols = (
        jnp.arange(NS)[:, None] == (state_index * local_rows + jnp.arange(local_rows))[None, :]
    ).astype(jnp.float32)

    def compose(carry, inputs):
        product, vector = carry
        matrix, shift_term = inputs
        product = split_product(matrix, product)
        vector = split_product(matrix, vector) + shift_term
        return ((product, vector), None)

    (column_product, span_offset), _ = lax.scan(
        compose, (start_cols, jnp.zeros((NS,), jnp.float32)), (full_elements, full_offsets)
    )
    span_matrix = lax.all_gather(column_product, "state", axis=1, tiled=True)

    def combine(earlier, later):
        return (
            jnp.dot(later[0], earlier[0], precision=HIGHEST),
            jnp.dot(later[0], earlier[1], precision=HIGHEST) + later[1],
        )

    identity = (jnp.eye(NS, dtype=jnp.float32), jnp.zeros((NS,), jnp.float32))
    before = prefix((span_matrix, span_offset), "tm", combine, identity)
    entry = jnp.dot(before[0], prior, precision=HIGHEST) + before[1]

    def sweep(current, inputs):
        matrix, shift_term = inputs
        new_mean = split_product(matrix, current) + shift_term
        return (new_mean, lax.dynamic_slice_in_dim(new_mean, state_index * local_rows, local_rows))

    _, filtered = lax.scan(sweep, entry, (full_elements, full_offsets))
    return filtered


def solution(mesh):
    return jax.shard_map(
        body,
        mesh=mesh,
        in_specs=(
            P("tm", "state", None),
            P("tm", "state", None, None),
            P("tm", None),
            P("tm", None, None),
            P("tm"),
            P("tm", None),
            P("tm", "state", None),
            P("tm", "state"),
            P(),
        ),
        out_specs=P("tm", "state"),
        check_vma=False,
    )
```

profile of v0, /device:TPU:1, one launch (start us, length us, event | category | flops | bytes accessed | tf_op | source)
XLA Modules:
  0.0 967.0 jit_solution(8072769552737119339)
XLA Ops:
  6.5 4.6 copy.27
  11.1 7.2 copy.28
  18.4 10.6 %fusion.58 = (bf16[32,2,64,8,64]{4,3,2,1,0:T(8,128)(2,1)}, f32[32,2,64,8,64]{4,3,2,1,0:T(8,128)}) fusion(bf16[32,2,64,3,64]{4,3,2,1,0:T(4,128)(2,1)} %copy.28, s32[32,2,3]{2,1,0:T(2,128)S(1)} %copy.26), kind=kOutput, calls=%fused_computation.79 | convolution fusion | flops 14681600 | bytes 14156544 | tf_op jit(solution)/shard_map/tikc,tiakb->tiacb/dot_general | solution.py:46
  29.0 11.9 %convert_element_type.81 = bf16[32,2,64,512]{3,2,1,0:T(8,128)(2,1)} reshape(bf16[32,2,64,8,64]{4,3,2,1,0:T(8,128)(2,1)} %get-tuple-element.329) | data formatting | bytes 8388608 | tf_op jit(solution)/shard_map/convert_element_type | solution.py:48
  41.4 8.8 convolution_convert_fusion
  50.2 3.2 fusion.39
  53.4 6.4 copy.33
  59.9 14.6 %reshape_reshape.3 = f32[32,128,512]{2,1,0:T(8,128)} reshape(f32[32,2,64,8,64]{4,3,2,1,0:T(8,128)} %get-tuple-element.330) | data formatting | bytes 16777216 | tf_op jit(solution)/shard_map/reshape;reshape | solution.py:83
  74.6 9.0 copy.34
  83.7 72.4 %all-reduce.2.cloned.1.call-done = bf16[32,128,512]{1,2,0:T(8,128)(2,1)} async-done(((bf16[32,128,512]{1,2,0:T(8,128)(2,1)}), bf16[32,128,512]{1,2,0:T(8,128)(2,1)}) %all-reduce.2.cloned.1.call-update) | async-done | bytes 4194320 | tf_op jit(solution)/shard_map/psum | solution.py:73
  156.1 7.9 fusion.30
  165.5 6.6 psum.15
  173.9 9.6 all_gather.22
  183.5 138.3 %all-gather.7.cloned.1.call-done = bf16[32,512,512]{1,2,0:T(8,128)(2,1)} async-done(((bf16[32,128,512]{1,2,0:T(8,128)(2,1)}), bf16[32,512,512]{1,2,0:T(8,128)(2,1)}) %all-gather.7.cloned.1.call-update) | async-done | bytes 16777232 | tf_op jit(solution)/shard_map/all_gather | solution.py:87
  321.8 22.6 %copy.35 = bf16[32,512,512]{2,1,0:T(8,128)(2,1)} copy(bf16[32,512,512]{1,2,0:T(8,128)(2,1)} %all-gather.7.cloned.1.call-done) | data formatting | bytes 33554432
  344.4 173.2 %while.47 = (s32[]{:T(128)}, f32[512,128]{1,0:T(8,128)S(1)}, f32[512]{0:T(512)S(1)}, bf16[32,512,512]{2,1,0:T(8,128)(2,1)}, f32[32,512]{1,0:T(8,128)S(1)}) while((s32[]{:T(128)}, f32[512,128]{1,0:T(8,128)S(1)}, f32[512]{0:T(512)S(1)}, bf16[32,512,512]{2,1,0:T(8,128)(2,1)}, f32[32,512]{1,0:T(8,128)S(1)}) %tuple.85), condition=%wide.region_3.4_spmd.clone.clone, body=%wide.region_2.3_spmd.clone.sunk.clone | while | flops 135597568 | bytes 4357196 | solution.py:100
  518.4 26.3 %all-gather.9.cloned.1.call-done = f32[512,512]{1,0:T(8,128)} async-done(((f32[512,128]{1,0:T(8,128)}), f32[512,512]{1,0:T(8,128)}) %all-gather.9.cloned.1.call-update) | async-done | bytes 1048592 | tf_op jit(solution)/shard_map/all_gather | solution.py:103
  544.9 25.7 %all-gather.2 = f32[32,1,512]{2,1,0:T(1,128)S(1)} all-gather(f32[1,1,512]{2,1,0:T(1,128)S(1)} %bitcast.166), channel_id=3, replica_groups=mesh['tm'=32,'state'=4] {'tm'}, dimensions={0}, use_global_device_ids=true | all-gather | bytes 67584 | tf_op jit(solution)/shard_map/all_gather | solution.py:17
  570.6 92.8 %all-gather.11.cloned.1.call-done = f32[16384,512]{1,0:T(8,128)} async-done(((f32[512,512]{1,0:T(8,128)}), f32[16384,512]{1,0:T(8,128)}) %all-gather.11.cloned.1.call-update) | async-done | bytes 33554448 | tf_op jit(solution)/shard_map/all_gather | solution.py:17
  663.4 168.3 %while.48 = (s32[]{:T(128)}, f32[512,512]{1,0:T(8,128)S(1)}, f32[512]{0:T(512)S(1)}, s32[]{:T(128)}, f32[32,512,512]{2,1,0:T(8,128)}, /*index=5*/f32[32,512]{1,0:T(8,128)S(1)}) while((s32[]{:T(128)}, f32[512,512]{1,0:T(8,128)S(1)}, f32[512]{0:T(512)S(1)}, s32[]{:T(128)}, f32[32,512,512]{2,1,0:T(8,128)}, ...), condition=%wide.region_5.6_spmd.clone.clone, body=%wide.region_4.5_spmd.clone.sunk.clone | while | flops 1614022656 | bytes 7361631 | solution.py:26
  703.7 3.1 convolution_select_fusion.3
  709.2 3.1 convolution_select_fusion.3
  736.3 3.1 convolution_select_fusion.3
  832.7 127.8 %while.46 = (s32[]{:T(128)}, f32[512]{0:T(512)S(1)}, f32[32,128]{1,0:T(8,128)}, bf16[32,512,512]{2,1,0:T(8,128)(2,1)}, f32[32,512]{1,0:T(8,128)S(1)}, /*index=5*/s32[]{:T(128)}) while((s32[]{:T(128)}, f32[512]{0:T(512)S(1)}, f32[32,128]{1,0:T(8,128)}, bf16[32,512,512]{2,1,0:T(8,128)(2,1)}, f32[32,512]{1,0:T(8,128)S(1)}, ...), condition=%wide.region_7.8_spmd.clone, body=%wide.region_6.7_spmd.sunk.clone | while | flops 1051650 | bytes 1081425 | solution.py:120
  (935 shorter events, 461.8 us)
Async XLA Ops:
  6.5 149.5 %copy-start = (bf16[32,128,128]{2,1,0:T(8,128)(2,1)S(1)}, bf16[32,128,128]{2,1,0:T(8,128)(2,1)}, u32[]{:S(2)}) copy-start(bf16[32,128,128]{2,1,0:T(8,128)(2,1)} %param.21) | copy-start | bytes 3145732
  6.5 11.7 %copy-start.5 = (s32[32,2,3]{0,1,2:T(2,128)S(1)}, s32[32,2,3]{0,1,2:T(2,128)}, u32[]{:S(2)}) copy-start(s32[32,2,3]{0,1,2:T(2,128)} %param.15) | copy-start | bytes 2308
  6.5 149.5 %all-reduce.2.cloned.1.call-start = ((), (), s32[]{:S(2)}) async-start(), calls=%async_computation | async-start | bytes 8388608 | tf_op jit(solution)/shard_map/psum | solution.py:73
  29.0 11.9 %copy-start.8 = (s32[32,2]{0,1:T(2,128)S(1)}, s32[32,2]{0,1:T(2,128)}, u32[]{:S(2)}) copy-start(s32[32,2]{0,1:T(2,128)} %param.17) | copy-start | bytes 772
  29.0 12.0 %copy-start.2 = (bf16[32,64,128]{2,1,0:T(8,128)(2,1)S(1)}, bf16[32,64,128]{2,1,0:T(8,128)(2,1)}, u32[]{:S(2)}) copy-start(bf16[32,64,128]{2,1,0:T(8,128)(2,1)} %param.18) | copy-start | bytes 1572868
  59.9 261.9 %all-gather.7.cloned.1.call-start = ((), (), s32[]{:S(2)}) async-start(), calls=%async_computation.1 | async-start | bytes 20971520 | tf_op jit(solution)/shard_map/all_gather | solution.py:87
  74.6 9.0 copy-start.7
  83.7 80.3 %copy-start.3 = (f32[32,128]{1,0:T(8,128)S(1)}, f32[32,128]{1,0:T(8,128)}, u32[]{:S(2)}) copy-start(f32[32,128]{1,0:T(8,128)} %param.22) | copy-start | bytes 49156
  83.7 88.4 %copy-start.4 = (f32[32,128]{1,0:T(8,128)S(1)}, f32[32,128]{1,0:T(8,128)}, u32[]{:S(2)}) copy-start(f32[32,128]{1,0:T(8,128)} %param.20) | copy-start | bytes 49156
  164.0 380.8 %all-gather.9.cloned.1.call-start = ((), (), s32[]{:S(2)}) async-start(), calls=%async_computation.2 | async-start | bytes 1310720 | tf_op jit(solution)/shard_map/all_gather | solution.py:103
  517.7 0.7 copy-start.1
  518.4 145.0 %all-gather.11.cloned.1.call-start = ((), (), s32[]{:S(2)}) async-start(), calls=%async_computation.3 | async-start | bytes 34603008 | tf_op jit(solution)/shard_map/all_gather | solution.py:17
  663.4 168.3 %copy-start.6 = (f32[512]{0:T(512)S(1)}, f32[512]{0:T(512)}, u32[]{:S(2)}) copy-start(f32[512]{0:T(512)} %param.23) | copy-start | bytes 6148
Sparse Core Ops, SparseCore 0:
  60.0 96.0 all-reduce.1
  164.1 157.6 all-gather.6
  518.5 26.1 all-gather.8
  547.1 116.2 all-gather.10
where the time goes:
time: 981 us; the launch traced here: 967 us
  matrix products  448 us (46%)
  waiting for transfers between devices  330 us (34%)
  local copies, waits for them, and re-layouts  126 us (13%)
  blocking collectives  41.9 us (4%)
  between operations  13.3 us (1%)
    all_gather x1, waiting for transfers between devices, body(): full_elements = lax.all_gather(element, 'state', axis=1, tiled=True)  138 us
    dot_general x96, matrix products, split_product(): jnp.dot(matrix, leading, preferred_element_type=jnp.float32)  126 us
    dot_general x96, matrix products, split_product(): jnp.dot(matrix, remainder, preferred_element_type=jnp.float32)  125 us
    dot_general x31, matrix products, combine(): jnp.dot(later[0], earlier[0], precision=HIGHEST)  95.1 us
    all_gather x1, waiting for transfers between devices, prefix(): pieces = jax.tree.map(lambda part: lax.all_gather(part, axis), value)  92.8 us
    psum x1, waiting for transfers between devices, body(): lax.psum(image_part.astype(jnp.bfloat16), 'state').astype(jnp.float32)  72.4 us
    dot_general x31, matrix products, combine(): jnp.dot(later[0], earlier[1], precision=HIGHEST) + later[1]  68.3 us
    dynamic_update_slice x32, local copies, waits for them, and re-layouts, body(): _, filtered = lax.scan(sweep, entry, (full_elements, full_offsets))  41.3 us
  transfers between devices with their start and end apart: 4, of which 4 were waited for; matrix products, arithmetic and copies ran while one was open for 3% of the time, Pallas kernels for 0%

commit v1 on v0

--- a/solution.py
+++ b/solution.py
@@ -10,6 +10,19 @@
 NB = 8
 OB = 2
 HIGHEST = lax.Precision.HIGHEST
+
+
+def collect(x, axis, dim):
+    size, index, span = (lax.axis_size(axis), lax.axis_index(axis), x.shape[dim])
+    right = [(i, (i + 1) % size) for i in range(size)]
+    whole = jnp.zeros((*x.shape[:dim], size * span, *x.shape[dim + 1 :]), x.dtype)
+    held = x
+    for step in range(size):
+        source = (index - step) % size
+        whole = lax.dynamic_update_slice_in_dim(whole, held, source * span, axis=dim)
+        if step < size - 1:
+            held = lax.ppermute(held, axis, right)
+    return whole
 
 
 def prefix(value, axis, join, neutral):
@@ -100,7 +113,7 @@
     (column_product, span_offset), _ = lax.scan(
         compose, (start_cols, jnp.zeros((NS,), jnp.float32)), (full_elements, full_offsets)
     )
-    span_matrix = lax.all_gather(column_product, "state", axis=1, tiled=True)
+    span_matrix = collect(column_product, "state", 1)
 
     def combine(earlier, later):
         return (

time: 981 us -> 975 us (level)
  waiting for transfers between devices: 330 us -> 319 us
    all_gather x1 -> x0, waiting for transfers between devices: 26.3 us -> none  [body(): span_matrix = lax.all_gather(column_product, 'state', axis=1, tiled=True)]
    ppermute x0 -> x3, waiting for transfers between devices: none -> 20.1 us  [collect(): held = lax.ppermute(held, axis, right)]
  transfers between devices with their start and end apart: 4 -> 6, of which waited for: 4 -> 6; matrix products, arithmetic and copies ran while one was open for 3% -> 3% of each run, Pallas kernels for 0% -> 0%
where the time goes in v1:
time: 975 us; the launch traced here: 960 us
  matrix products  448 us (46%)
  waiting for transfers between devices  319 us (33%)
  local copies, waits for them, and re-layouts  127 us (13%)
  blocking collectives  45.2 us (5%)
  between operations  13.3 us (1%)
    all_gather x1, waiting for transfers between devices, body(): full_elements = lax.all_gather(element, 'state', axis=1, tiled=True)  138 us
    dot_general x96, matrix products, split_product(): jnp.dot(matrix, leading, preferred_element_type=jnp.float32)  126 us
    dot_general x96, matrix products, split_product(): jnp.dot(matrix, remainder, preferred_element_type=jnp.float32)  125 us
    dot_general x31, matrix products, combine(): jnp.dot(later[0], earlier[0], precision=HIGHEST)  95.1 us
    all_gather x1, waiting for transfers between devices, prefix(): pieces = jax.tree.map(lambda part: lax.all_gather(part, axis), value)  88.4 us
    psum x1, waiting for transfers between devices, body(): lax.psum(image_part.astype(jnp.bfloat16), 'state').astype(jnp.float32)  72.4 us
    dot_general x31, matrix products, combine(): jnp.dot(later[0], earlier[1], precision=HIGHEST) + later[1]  68.3 us
    dynamic_update_slice x32, local copies, waits for them, and re-layouts, body(): _, filtered = lax.scan(sweep, entry, (full_elements, full_offsets))  41.3 us
  transfers between devices with their start and end apart: 6, of which 6 were waited for; matrix products, arithmetic and copies ran while one was open for 3% of the time, Pallas kernels for 0%

profile of v1, /device:TPU:1, one launch (start us, length us, event | category | flops | bytes accessed | tf_op | source)
XLA Modules:
  0.0 960.3 jit_solution(1751004534365124944)
XLA Ops:
  6.5 4.6 copy.27
  11.1 7.2 copy.28
  18.4 10.6 %fusion.58 = (bf16[32,2,64,8,64]{4,3,2,1,0:T(8,128)(2,1)}, f32[32,2,64,8,64]{4,3,2,1,0:T(8,128)}) fusion(bf16[32,2,64,3,64]{4,3,2,1,0:T(4,128)(2,1)} %copy.28, s32[32,2,3]{2,1,0:T(2,128)S(1)} %copy.26), kind=kOutput, calls=%fused_computation.83 | convolution fusion | flops 14681600 | bytes 14156544 | tf_op jit(solution)/shard_map/tikc,tiakb->tiacb/dot_general | solution.py:59
  29.0 11.9 %convert_element_type.81 = bf16[32,2,64,512]{3,2,1,0:T(8,128)(2,1)} reshape(bf16[32,2,64,8,64]{4,3,2,1,0:T(8,128)(2,1)} %get-tuple-element.329) | data formatting | bytes 8388608 | tf_op jit(solution)/shard_map/convert_element_type | solution.py:61
  41.4 8.8 convolution_convert_fusion
  50.2 3.2 fusion.39
  53.4 6.4 copy.33
  59.9 14.6 %reshape_reshape.3 = f32[32,128,512]{2,1,0:T(8,128)} reshape(f32[32,2,64,8,64]{4,3,2,1,0:T(8,128)} %get-tuple-element.330) | data formatting | bytes 16777216 | tf_op jit(solution)/shard_map/reshape;reshape | solution.py:96
  74.6 9.0 copy.34
  83.7 72.4 %all-reduce.2.cloned.1.call-done = bf16[32,128,512]{1,2,0:T(8,128)(2,1)} async-done(((bf16[32,128,512]{1,2,0:T(8,128)(2,1)}), bf16[32,128,512]{1,2,0:T(8,128)(2,1)}) %all-reduce.2.cloned.1.call-update) | async-done | bytes 4194320 | tf_op jit(solution)/shard_map/psum | solution.py:86
  156.1 7.9 fusion.30
  165.5 6.6 psum.15
  173.9 9.6 all_gather.28
  183.5 138.3 %all-gather.5.cloned.1.call-done = bf16[32,512,512]{1,2,0:T(8,128)(2,1)} async-done(((bf16[32,128,512]{1,2,0:T(8,128)(2,1)}), bf16[32,512,512]{1,2,0:T(8,128)(2,1)}) %all-gather.5.cloned.1.call-update) | async-done | bytes 16777232 | tf_op jit(solution)/shard_map/all_gather | solution.py:100
  321.8 22.6 %copy.35 = bf16[32,512,512]{2,1,0:T(8,128)(2,1)} copy(bf16[32,512,512]{1,2,0:T(8,128)(2,1)} %all-gather.5.cloned.1.call-done) | data formatting | bytes 33554432
  344.4 173.2 %while.47 = (s32[]{:T(128)}, f32[512,128]{1,0:T(8,128)S(1)}, f32[512]{0:T(512)S(1)}, bf16[32,512,512]{2,1,0:T(8,128)(2,1)}, f32[32,512]{1,0:T(8,128)S(1)}) while((s32[]{:T(128)}, f32[512,128]{1,0:T(8,128)S(1)}, f32[512]{0:T(512)S(1)}, bf16[32,512,512]{2,1,0:T(8,128)(2,1)}, f32[32,512]{1,0:T(8,128)S(1)}) %tuple.85), condition=%wide.region_3.4_spmd.clone.clone, body=%wide.region_2.3_spmd.clone.sunk.clone | while | flops 135597568 | bytes 4357196 | solution.py:113
  517.7 7.5 collective-permute-done
  525.4 6.3 collective-permute-done.1
  531.7 6.4 collective-permute-done.2
  539.3 29.0 %all-gather.1 = f32[32,1,512]{2,1,0:T(1,128)S(1)} all-gather(f32[1,1,512]{2,1,0:T(1,128)S(1)} %bitcast.172), channel_id=2, replica_groups=mesh['tm'=32,'state'=4] {'tm'}, dimensions={0}, use_global_device_ids=true | all-gather | bytes 67584 | tf_op jit(solution)/shard_map/all_gather | solution.py:30
  568.3 88.4 %all-gather.7.cloned.1.call-done = f32[32,512,512]{2,1,0:T(8,128)} async-done(((f32[1,512,512]{2,1,0:T(8,128)}), f32[32,512,512]{2,1,0:T(8,128)}) %all-gather.7.cloned.1.call-update) | async-done | bytes 33554448 | tf_op jit(solution)/shard_map/all_gather | solution.py:30
  656.6 168.3 %while.48 = (s32[]{:T(128)}, f32[512,512]{1,0:T(8,128)S(1)}, f32[512]{0:T(512)S(1)}, s32[]{:T(128)}, f32[32,512,512]{2,1,0:T(8,128)}, /*index=5*/f32[32,512]{1,0:T(8,128)S(1)}) while((s32[]{:T(128)}, f32[512,512]{1,0:T(8,128)S(1)}, f32[512]{0:T(512)S(1)}, s32[]{:T(128)}, f32[32,512,512]{2,1,0:T(8,128)}, ...), condition=%wide.region_5.6_spmd.clone.clone, body=%wide.region_4.5_spmd.clone.sunk.clone | while | flops 1614022656 | bytes 7361631 | solution.py:39
  664.4 3.1 convolution_select_fusion.3
  826.0 127.8 %while.46 = (s32[]{:T(128)}, f32[512]{0:T(512)S(1)}, f32[32,128]{1,0:T(8,128)}, bf16[32,512,512]{2,1,0:T(8,128)(2,1)}, f32[32,512]{1,0:T(8,128)S(1)}, /*index=5*/s32[]{:T(128)}) while((s32[]{:T(128)}, f32[512]{0:T(512)S(1)}, f32[32,128]{1,0:T(8,128)}, bf16[32,512,512]{2,1,0:T(8,128)(2,1)}, f32[32,512]{1,0:T(8,128)S(1)}, ...), condition=%wide.region_7.8_spmd.clone, body=%wide.region_6.7_spmd.sunk.clone | while | flops 1051650 | bytes 1081425 | solution.py:133
  (943 shorter events, 468.5 us)
Async XLA Ops:
  6.5 149.5 %copy-start = (bf16[32,128,128]{2,1,0:T(8,128)(2,1)S(1)}, bf16[32,128,128]{2,1,0:T(8,128)(2,1)}, u32[]{:S(2)}) copy-start(bf16[32,128,128]{2,1,0:T(8,128)(2,1)} %param.21) | copy-start | bytes 3145732
  6.5 11.7 %copy-start.5 = (s32[32,2,3]{0,1,2:T(2,128)S(1)}, s32[32,2,3]{0,1,2:T(2,128)}, u32[]{:S(2)}) copy-start(s32[32,2,3]{0,1,2:T(2,128)} %param.15) | copy-start | bytes 2308
  6.5 149.5 %all-reduce.2.cloned.1.call-start = ((), (), s32[]{:S(2)}) async-start(), calls=%async_computation | async-start | bytes 8388608 | tf_op jit(solution)/shard_map/psum | solution.py:86
  29.0 11.9 %copy-start.8 = (s32[32,2]{0,1:T(2,128)S(1)}, s32[32,2]{0,1:T(2,128)}, u32[]{:S(2)}) copy-start(s32[32,2]{0,1:T(2,128)} %param.17) | copy-start | bytes 772
  29.0 12.0 %copy-start.2 = (bf16[32,64,128]{2,1,0:T(8,128)(2,1)S(1)}, bf16[32,64,128]{2,1,0:T(8,128)(2,1)}, u32[]{:S(2)}) copy-start(bf16[32,64,128]{2,1,0:T(8,128)(2,1)} %param.18) | copy-start | bytes 1572868
  59.9 261.9 %all-gather.5.cloned.1.call-start = ((), (), s32[]{:S(2)}) async-start(), calls=%async_computation.1 | async-start | bytes 20971520 | tf_op jit(solution)/shard_map/all_gather | solution.py:100
  74.6 9.0 copy-start.7
  83.7 80.3 %copy-start.3 = (f32[32,128]{1,0:T(8,128)S(1)}, f32[32,128]{1,0:T(8,128)}, u32[]{:S(2)}) copy-start(f32[32,128]{1,0:T(8,128)} %param.22) | copy-start | bytes 49156
  83.7 88.4 %copy-start.4 = (f32[32,128]{1,0:T(8,128)S(1)}, f32[32,128]{1,0:T(8,128)}, u32[]{:S(2)}) copy-start(f32[32,128]{1,0:T(8,128)} %param.20) | copy-start | bytes 49156
  164.0 492.7 %all-gather.7.cloned.1.call-start = ((), (), s32[]{:S(2)}) async-start(), calls=%async_computation.2 | async-start | bytes 34603008 | tf_op jit(solution)/shard_map/all_gather | solution.py:30
  517.7 7.5 collective-permute-start
  525.2 6.4 collective-permute-start.1
  531.6 6.4 collective-permute-start.2
  538.1 1.0 copy-start.1
  656.6 168.3 %copy-start.6 = (f32[512]{0:T(512)S(1)}, f32[512]{0:T(512)}, u32[]{:S(2)}) copy-start(f32[512]{0:T(512)} %param.23) | copy-start | bytes 6148
Sparse Core Ops, SparseCore 0:
  60.0 96.0 all-reduce.1
  164.1 157.6 all-gather.4
  539.2 117.3 all-gather.6
